TPU v7x, 1024 devices: a whole 4x8x16 slice. The times are simulated.
1024 devices in a mesh: dp: 16 (over y, core), table: 64 (over x, z).
Axes of the slice: x: 4, y: 8, z: 16, core: 2. Of those that a mesh axis runs over, the one named last changes fastest.
Arguments:
- queries: bfloat16 [524288, 256], P(('dp', 'table')), may hold values from -6 to 6
- item_rows: bfloat16 [262144, 256], P(('dp', 'table')), may hold values from -1.5 to 1.5
- item_bin: int32 [262144], P(('dp', 'table')), may hold values from 0 to 127
- counts: int32 [1024], P(('dp', 'table')), may hold values from 128 to 256, as said below
- labels: int32 [524288], P(('dp', 'table')), may hold values from 0 to 255, as said below
- owner: int32 [262144], P(('dp', 'table')), may hold values from 0 to 1023, as said below
- local_row: int32 [262144], P(('dp', 'table')), may hold values from 0 to 2047
- logq: float32 [128], replicated, may hold values from -6 to 0
- tower_weight: bfloat16 [256, 256], replicated, may hold values from -0.375 to 0.375
- tower_gain: float32 [256], replicated, may hold values from 0.25 to 1.75
Outputs:
- grad_query: bfloat16 [524288, 256], P(('dp', 'table'))
- grad_table: float32 [2097152, 256], P(('dp', 'table'))
- grad_weight: float32 [256, 256], replicated
- grad_gain: float32 [256], replicated
Inputs may be any that keep to these rules, and one draw needn't show every extreme that they name: `counts`: each device's count of live slots; some device has all 256 live. `labels`: a query's positive is a live slot of its own device. owner = dp index * 64 + table index of the owning device. Among the 256 slots of one device at most 32 name owners of one dp index, reached on every device. Take the slots of all devices of one table index t whose owners have dp index a, each device's in slot order, device after device in dp order, the j-th of device b at position b * 32 + j: at most 8 of them name one table index, and this is reached.
All inputs are finite; a program needn't handle non-finite values.
Results may differ from a plain program's by a relative error of at most 0.012.
Values may be sent and summed in bfloat16 or wider, within the bound.
A program may use at most 64 MiB of HBM per device.

v0:
```python
import jax
import jax.numpy as jnp
from jax import lax
from jax.sharding import PartitionSpec as P

ROWS_DEV = 2048


NEG = -1e30
TEMP = 0.05


def lookup(bins, logq):
    hits = bins[:, None] == jnp.arange(logq.shape[0], dtype=jnp.int32)[None, :]
    return jnp.sum(jnp.where(hits, logq[None, :], jnp.float32(0.0)), axis=1)


def bucket_place(target, buckets):
    hits = (target[:, None] == jnp.arange(buckets, dtype=jnp.int32)[None, :]).astype(jnp.int32)
    before = jnp.cumsum(hits, axis=0) - hits
    return jnp.sum(before * hits, axis=1)


def body(
    queries, item_rows, item_bin, counts, labels, owner, local_row, logq, tower_weight, tower_gain
):
    q_rows = queries.shape[0]
    u_rows = item_rows.shape[0]
    width = item_rows.shape[1]
    rows_f = item_rows.astype(jnp.float32)
    items = (
        tower_gain[None, :] * rows_f
        + jnp.dot(item_rows, tower_weight, preferred_element_type=jnp.float32)
    ).astype(jnp.bfloat16)
    my_group = lax.axis_index("dp")
    group_v, group_bins, group_counts = (
        lax.all_gather(items, "dp", axis=0, tiled=True),
        lax.all_gather(item_bin, "dp", axis=0, tiled=True),
        lax.all_gather(counts, "dp", axis=0, tiled=True),
    )
    slot = jnp.arange(group_v.shape[0], dtype=jnp.int32)
    live = slot % u_rows < jnp.repeat(group_counts, u_rows, total_repeat_length=group_v.shape[0])
    scores = (
        jnp.dot(queries, group_v.T, preferred_element_type=jnp.float32) / TEMP
        - lookup(group_bins, logq)[None, :]
    )
    scores = jnp.where(live[None, :], scores, NEG)
    top = jnp.max(scores, axis=1, keepdims=True)
    weight = jnp.exp(scores - top)
    prob = weight / jnp.sum(weight, axis=1, keepdims=True)
    target = my_group * u_rows + labels
    onehot = (slot[None, :] == target[:, None]).astype(jnp.float32)
    logit_grad = ((prob - onehot) / TEMP).astype(jnp.bfloat16)
    grad_query = jnp.dot(logit_grad, group_v, preferred_element_type=jnp.float32).astype(
        jnp.bfloat16
    )
    block = lax.slice_in_dim(logit_grad, 0, u_rows * lax.axis_size("dp"), axis=1)
    item_grad = lax.psum_scatter(
        lax.dot_general(
            block, queries, (((0,), (0,)), ((), ())), preferred_element_type=jnp.float32
        ),
        "dp",
        scatter_dimension=0,
        tiled=True,
    )
    item_grad_b = item_grad.astype(jnp.bfloat16)
    weight_part = lax.dot_general(
        item_rows, item_grad_b, (((0,), (0,)), ((), ())), preferred_element_type=jnp.float32
    )
    gain_part = jnp.sum(item_grad * rows_f, axis=0)
    weight_sum, gain_sum = lax.psum((weight_part, gain_part), ("dp", "table"))
    n_dp = lax.axis_size("dp")
    n_tab = lax.axis_size("table")
    queries_all = q_rows * n_dp * n_tab
    grad_weight = weight_sum / queries_all
    grad_gain = gain_sum / queries_all
    row_grad = (
        tower_gain[None, :] * item_grad
        + lax.dot_general(
            item_grad_b, tower_weight, (((1,), (1,)), ((), ())), preferred_element_type=jnp.float32
        )
    ).astype(jnp.bfloat16)
    cap_dp = max(2, 2 * u_rows // n_dp)
    cap_tab = max(2, (n_dp * cap_dp + n_tab - 1) // n_tab)
    owner_dp = owner // n_tab
    owner_tab = owner % n_tab
    first_place = bucket_place(owner_dp, n_dp)
    first_grad = (
        jnp.zeros((n_dp, cap_dp, width), jnp.bfloat16).at[owner_dp, first_place].set(row_grad)
    )
    first_rows = (
        jnp.full((n_dp, cap_dp), ROWS_DEV, jnp.int32).at[owner_dp, first_place].set(local_row)
    )
    first_tab = jnp.full((n_dp, cap_dp), n_tab, jnp.int32).at[owner_dp, first_place].set(owner_tab)
    mid_grad, mid_rows, mid_tab = (
        lax.all_to_all(first_grad, "dp", split_axis=0, concat_axis=0, tiled=True),
        lax.all_to_all(first_rows, "dp", split_axis=0, concat_axis=0, tiled=True),
        lax.all_to_all(first_tab, "dp", split_axis=0, concat_axis=0, tiled=True),
    )
    mid_grad = mid_grad.reshape(n_dp * cap_dp, width)
    mid_rows = mid_rows.reshape(-1)
    mid_tab = mid_tab.reshape(-1)
    second_place = bucket_place(mid_tab, n_tab)
    second_grad = (
        jnp.zeros((n_tab, cap_tab, width), jnp.bfloat16)
        .at[mid_tab, second_place]
        .set(mid_grad, mode="drop")
    )
    second_rows = (
        jnp.full((n_tab, cap_tab), ROWS_DEV, jnp.int32)
        .at[mid_tab, second_place]
        .set(mid_rows, mode="drop")
    )
    got_grad, got_rows = (
        lax.all_to_all(second_grad, "table", split_axis=0, concat_axis=0, tiled=True),
        lax.all_to_all(second_rows, "table", split_axis=0, concat_axis=0, tiled=True),
    )
    grad_table = (
        jnp.zeros((ROWS_DEV, width), jnp.float32)
        .at[got_rows.reshape(-1)]
        .add(got_grad.reshape(-1, width).astype(jnp.float32), mode="drop")
    )
    return (grad_query, grad_table, grad_weight, grad_gain)


def solution(mesh):
    return jax.shard_map(
        body,
        mesh=mesh,
        in_specs=(
            P(("dp", "table"), None),
            P(("dp", "table"), None),
            P(("dp", "table")),
            P(("dp", "table")),
            P(("dp", "table")),
            P(("dp", "table")),
            P(("dp", "table")),
            P(),
            P(),
            P(),
        ),
        out_specs=(P(("dp", "table"), None), P(("dp", "table"), None), P(), P()),
        check_vma=False,
    )
```

profile of v0, /device:TPU:1, one launch (start us, length us, event | category | flops | bytes accessed | tf_op | source)
XLA Modules:
  0.0 825.8 jit_solution(13822508679647494406)
XLA Ops:
  11.9 16.3 %all-reduce = s32[16]{0:T(128)S(1)} all-reduce(s32[16]{0:T(128)S(1)} %dynamic-update-slice.3), channel_id=1, replica_groups=mesh['dp'=16,'table'=64] {'dp'}, use_global_device_ids=true, to_apply=%add | all-reduce | flops 16 | bytes 128
  28.2 25.6 %all-gather = s32[16,1,256]{2,1,0:T(1,128)S(1)} all-gather(s32[1,1,256]{2,1,0:T(1,128)} %bitcast.112), channel_id=1, replica_groups=mesh['dp'=16,'table'=64] {'dp'}, dimensions={0}, use_global_device_ids=true | all-gather | bytes 17408 | tf_op jit(solution)/shard_map/all_gather | solution.py:38
  54.6 1.9 select_reduce_fusion
  57.2 10.9 %fusion.16 = pred[4096]{0:T(1024)(128)(4,1)S(1)} fusion(pred[4096]{0:T(1024)(128)(4,1)} %constant.294, pred[4096]{0:T(1024)(128)(4,1)} %constant.295, pred[4096]{0:T(1024)(128)(4,1)} %constant.296, pred[4096]{0:T(1024)(128)(4,1)} %constant.297, pred[4096]{0:T(1024)(128)(4,1)} %constant.298, pred[4096]{0:T(1024)(128)(4,1)} %constant.299, ...), kind=kLoop, calls=%fused_computation.41 | loop fusion | flops 90112 | bytes 65600 | tf_op jit(solution)/shard_map/lt | solution.py:42
  68.2 3.7 fusion.27
  73.1 2.6 fusion.1
  75.7 1.9 copy-done.1
  77.6 3.2 fusion.28
  83.1 35.4 %scatter_fusion = s32[16,32]{1,0:T(8,128)} fusion(s32[16,32]{1,0:T(8,128)} %broadcast_in_dim.48, s32[256]{0:T(256)S(1)} %bitcast.98, s32[256]{0:T(256)S(1)} %get-tuple-element.34), kind=kCustom, calls=%fused_computation | custom fusion | bytes 5120 | tf_op jit(solution)/shard_map/scatter | solution.py:94
  118.5 4.5 all-to-all-start
  123.6 35.4 %scatter_fusion.1 = s32[16,32]{1,0:T(8,128)} fusion(s32[16,32]{1,0:T(8,128)} %broadcast_in_dim.50, s32[256]{0:T(256)S(1)} %bitcast.99, s32[256]{0:T(256)S(1)} %copy-done.6), kind=kCustom, calls=%fused_computation.1 | custom fusion | bytes 5120 | tf_op jit(solution)/shard_map/scatter | solution.py:92
  159.0 7.3 all-to-all-start.1
  169.3 4.0 all-to-all-done.1
  174.2 22.3 %scatter_fusion.2 = s32[64,8]{0,1:T(8,128)S(1)} fusion(s32[64,8]{0,1:T(8,128)S(1)} %broadcast_in_dim.47, s32[512]{0:T(512)S(1)} %bitcast.101, s32[512]{0:T(512)S(1)} %reshape.297), kind=kCustom, calls=%fused_computation.2 | custom fusion | bytes 10240 | tf_op jit(solution)/shard_map/scatter | solution.py:112
  197.2 16.3 %all-to-all-start.2 = ((s32[64,1,8]{2,1,0:T(1,128)}), s32[64,1,8]{2,1,0:T(1,128)S(1)}, u32[]{:S(2)}, u32[]{:S(2)}) async-start(s32[64,1,8]{2,1,0:T(1,128)} %copy.29), calls=%async_computation.2 | async-start | bytes 65536 | tf_op jit(solution)/shard_map/all_to_all | solution.py:116
  215.6 29.6 %scatter_fusion.3 = bf16[16,32,256]{2,1,0:T(8,128)(2,1)} fusion(bf16[16,32,256]{2,1,0:T(8,128)(2,1)} %broadcast_in_dim.52, s32[256]{0:T(256)S(1)} %bitcast.100, bf16[256,256]{1,0:T(8,128)(2,1)S(1)} %fusion.4), kind=kCustom, calls=%fused_computation.3 | custom fusion | bytes 395264 | tf_op jit(solution)/shard_map/scatter | solution.py:89
  245.2 4.2 all-to-all-start.3
  250.2 11.0 %all-to-all-done.3 = bf16[16,32,256]{2,1,0:T(8,128)(2,1)S(1)} async-done(((bf16[16,32,256]{2,1,0:T(8,128)(2,1)}), bf16[16,32,256]{2,1,0:T(8,128)(2,1)S(1)}, u32[]{:S(2)}, u32[]{:S(2)}) %all-to-all-start.3) | async-done | bytes 262176 | tf_op jit(solution)/shard_map/all_to_all | solution.py:96
  262.0 56.2 %scatter_fusion.4 = bf16[64,8,256]{2,1,0:T(8,128)(2,1)} fusion(bf16[64,8,256]{2,1,0:T(8,128)(2,1)} %broadcast_in_dim.51, s32[512]{0:T(512)S(1)} %bitcast.102, bf16[512,256]{1,0:T(8,128)(2,1)S(1)} %bitcast.103), kind=kCustom, calls=%fused_computation.4 | custom fusion | bytes 790528 | tf_op jit(solution)/shard_map/scatter | solution.py:107
  318.2 14.8 %all-to-all-start.4 = ((bf16[64,8,256]{2,1,0:T(8,128)(2,1)}), bf16[64,8,256]{2,1,0:T(8,128)(2,1)S(1)}, u32[]{:S(2)}, u32[]{:S(2)}) async-start(bf16[64,8,256]{2,1,0:T(8,128)(2,1)} %scatter_fusion.4), calls=%async_computation.5 | async-start | bytes 524288 | tf_op jit(solution)/shard_map/all_to_all | solution.py:115
  333.1 4.2 convolution_convert_fusion
  338.4 122.2 %psum.15 = f32[256]{0:T(256)S(1)} all-reduce(f32[256]{0:T(256)S(1)} %fusion.8), channel_id=1, replica_groups=mesh['dp'=16,'table'=64] {'dp','table'}, use_global_device_ids=true, to_apply=%region_18.19 | all-reduce | flops 256 | bytes 2048 | tf_op jit(solution)/shard_map/psum | solution.py:71
  461.1 351.6 %all-reduce.3.cloned.1.call-done = f32[256,256]{0,1:T(8,128)} async-done(((f32[256,256]{0,1:T(8,128)}), f32[256,256]{0,1:T(8,128)}) %all-reduce.3.cloned.1.call-update) | async-done | bytes 262160 | tf_op jit(solution)/shard_map/psum | solution.py:71
  814.5 4.7 scatter_custom_fusion.5
  (72 shorter events, 20.9 us)
Async XLA Ops:
  7.2 61.0 %copy-start = (bf16[512,256]{1,0:T(8,128)(2,1)S(1)}, bf16[512,256]{1,0:T(8,128)(2,1)}, u32[]{:S(2)}) copy-start(bf16[512,256]{1,0:T(8,128)(2,1)} %param.12) | copy-start | bytes 786436
  7.2 61.0 %all-gather.3.cloned.1.call-start = ((), (), s32[]{:S(2)}) async-start(), calls=%async_computation.6 | async-start | bytes 2228224 | tf_op jit(solution)/shard_map/all_gather | solution.py:37
  9.2 204.4 %reduce-scatter.2.cloned.1.call-start = ((), (), s32[]{:S(2)}) async-start(), calls=%async_computation.7 | async-start | bytes 4456448 | tf_op jit(solution)/shard_map/reduce_scatter | solution.py:58
  75.7 1.9 copy-start.1
  80.9 0.7 copy-start.7
  80.9 42.8 %copy-start.6 = (s32[256]{0:T(256)S(1)}, s32[256]{0:T(256)}, u32[]{:S(2)}) copy-start(s32[256]{0:T(256)} %param.18) | copy-start | bytes 3076
  118.5 95.1 %copy-start.4 = (bf16[256,256]{1,0:T(8,128)(2,1)S(1)}, bf16[256,256]{1,0:T(8,128)(2,1)}, u32[]{:S(2)}) copy-start(bf16[256,256]{1,0:T(8,128)(2,1)} %param.20) | copy-start | bytes 393220
  118.5 95.1 %copy-start.5 = (f32[256]{0:T(256)S(1)}, f32[256]{0:T(256)}, u32[]{:S(2)}) copy-start(f32[256]{0:T(256)} %param.21) | copy-start | bytes 3076
  118.5 40.5 %all-to-all-start = ((s32[16,1,32]{2,1,0:T(1,128)}), s32[16,1,32]{2,1,0:T(1,128)S(1)}, u32[]{:S(2)}, u32[]{:S(2)}) async-start(s32[16,1,32]{2,1,0:T(1,128)} %bitcast.26), calls=%async_computation | async-start | bytes 16384 | tf_op jit(solution)/shard_map/all_to_all | solution.py:98
  159.0 14.3 %all-to-all-start.1 = ((s32[16,1,32]{2,1,0:T(1,128)}), s32[16,1,32]{2,1,0:T(1,128)S(1)}, u32[]{:S(2)}, u32[]{:S(2)}) async-start(s32[16,1,32]{2,1,0:T(1,128)} %bitcast.31), calls=%async_computation.1 | async-start | bytes 16384 | tf_op jit(solution)/shard_map/all_to_all | solution.py:97
  197.2 47.9 %all-to-all-start.2 = ((s32[64,1,8]{2,1,0:T(1,128)}), s32[64,1,8]{2,1,0:T(1,128)S(1)}, u32[]{:S(2)}, u32[]{:S(2)}) async-start(s32[64,1,8]{2,1,0:T(1,128)} %copy.29), calls=%async_computation.2 | async-start | bytes 65536 | tf_op jit(solution)/shard_map/all_to_all | solution.py:116
  215.6 117.5 %copy-start.8 = (bf16[4096,256]{1,0:T(8,128)(2,1)S(1)}, bf16[4096,256]{1,0:T(8,128)(2,1)}, u32[]{:S(2)}) copy-start(bf16[4096,256]{1,0:T(8,128)(2,1)} %all-gather.3.cloned.1.call-done) | copy-start | bytes 6291460
  245.2 16.1 %all-to-all-start.3 = ((bf16[16,32,256]{2,1,0:T(8,128)(2,1)}), bf16[16,32,256]{2,1,0:T(8,128)(2,1)S(1)}, u32[]{:S(2)}, u32[]{:S(2)}) async-start(bf16[16,32,256]{2,1,0:T(8,128)(2,1)} %scatter_fusion.3), calls=%async_computation.4 | async-start | bytes 524288 | tf_op jit(solution)/shard_map/all_to_all | solution.py:96
  318.2 496.4 %all-to-all-start.4 = ((bf16[64,8,256]{2,1,0:T(8,128)(2,1)}), bf16[64,8,256]{2,1,0:T(8,128)(2,1)S(1)}, u32[]{:S(2)}, u32[]{:S(2)}) async-start(bf16[64,8,256]{2,1,0:T(8,128)(2,1)} %scatter_fusion.4), calls=%async_computation.5 | async-start | bytes 524288 | tf_op jit(solution)/shard_map/all_to_all | solution.py:115
  333.0 4.3 copy-start.2
  333.0 4.3 copy-start.3
  333.0 479.7 %all-reduce.3.cloned.1.call-start = ((), (), s32[]{:S(2)}) async-start(), calls=%async_computation.8 | async-start | bytes 524288 | tf_op jit(solution)/shard_map/psum | solution.py:71
Sparse Core Ops, SparseCore 0:
  11.3 56.2 all-gather.2
  81.0 68.0 reduce-scatter.1
  339.9 472.7 all-reduce.2
where the time goes:
time: 832 us; the launch traced here: 826 us
  waiting for transfers between devices  367 us (44%)
  local copies, waits for them, and re-layouts  190 us (23%)
  blocking collectives  164 us (20%)
  starting transfers between devices  47.3 us (6%)
  other arithmetic  27.9 us (3%)
  matrix products  15.3 us (2%)
  between operations  14.6 us (2%)
    psum x1, waiting for transfers between devices, body(): weight_sum, gain_sum = lax.psum((weight_part, gain_part), ('dp', 'table'))  352 us
    psum x1, blocking collectives, body(): weight_sum, gain_sum = lax.psum((weight_part, gain_part), ('dp', 'table'))  122 us
    scatter x1, local copies, waits for them, and re-layouts, body(): second_grad = jnp.zeros((n_tab, cap_tab, width), jnp.bfloat16).at[mid_tab...  56.2 us
    scatter x1, local copies, waits for them, and re-layouts, body(): jnp.full((n_dp, cap_dp), ROWS_DEV, jnp.int32).at[owner_dp, first_place]  35.4 us
    scatter x1, local copies, waits for them, and re-layouts, body(): jnp.full((n_dp, cap_dp), n_tab, jnp.int32).at[owner_dp, first_place]  35.4 us
    scatter x1, local copies, waits for them, and re-layouts, body(): jnp.zeros((n_dp, cap_dp, width), jnp.bfloat16).at[owner_dp, first_place]  29.6 us
    all_gather x1, blocking collectives, body(): lax.all_gather(item_bin, 'dp', axis=0, tiled=True)  25.6 us
    scatter x1, local copies, waits for them, and re-layouts, body(): second_rows = jnp.full((n_tab, cap_tab), ROWS_DEV, jnp.int32).at[mid_tab,...  22.3 us
  transfers between devices with their start and end apart: 8, of which 3 were waited for; matrix products, arithmetic and copies ran while one was open for 19% of the time, Pallas kernels for 0%

commit v1 on v0

v1 whole, which is shorter than its diff:
```python
import functools
import math

import jax
import jax.numpy as jnp
from jax import lax
from jax.experimental import pallas as pl
from jax.experimental.pallas import tpu as pltpu
from jax.sharding import PartitionSpec as P

ROWS_DEV = 2048
NEG = -1e30
INV_TEMP = 20.0
SCALE2 = INV_TEMP * math.log2(math.e)
EXT = 16
CORES = 2
X_CHIPS = 4
MESH = pl.DeviceIdType.MESH
F32 = jnp.float32
BF16 = jnp.bfloat16


def iota(shape, dim):
    return lax.broadcasted_iota(jnp.int32, shape, dim)


def dot(a, b, da=1, db=0):
    return lax.dot_general(a, b, (((da,), (db,)), ((), ())), preferred_element_type=F32)


def split3(x):
    hi = x.astype(BF16).astype(F32)
    mid = (x - hi).astype(BF16).astype(F32)
    low = (x - hi - mid).astype(BF16).astype(F32)
    return hi, mid, low


def step_kernel(
    n_dp, n_x, n_z, cap_dp, cap_t,
    q_hbm, rows_hbm, bin_hbm, cnt_hbm, lab_hbm, own_hbm, loc_hbm, logq_hbm, w_hbm, gain_hbm,
    gq_hbm, got_hbm, code_hbm, gw_hbm, gg_hbm,
    q_ref, rows_ref, bin_ref, cnt_ref, lab_ref, own_ref, loc_ref, logq_ref, w_ref, gain_ref,
    gq_ref, got_ref, code_ref, gw_ref, gg_ref,
    blocks, weights, q_t, z_t, top, total, acc, sib_out, sib_in, ring_out, ring_in,
    mid_meta, base_ref, place, first, mid, second, got, meta_out, meta_in,
    w_out, w_in, x_in, r_out, r_in, row_in, full,
    in_sem, out_sem,
    ag_ring_send, ag_ring_recv, ag_sib_send, ag_sib_recv, rs_sib_send, rs_sib_recv, rs_ring_send, rs_ring_recv,
    all_send, all_recv,
):
    n_tab = n_x * n_z
    n_y = n_dp // CORES
    half = n_y // 2
    u_rows, width = rows_ref.shape
    q_rows = q_ref.shape[0]
    queries_all = q_rows * n_dp * n_tab
    cut = u_rows // 2 + EXT
    subs = (pl.ds(0, cut), pl.ds(cut, u_rows + EXT - cut))
    halves = (pl.ds(0, u_rows // 2), pl.ds(u_rows // 2, u_rows // 2))

    fetches = [
        pltpu.make_async_copy(src, dst, in_sem.at[k])
        for k, (src, dst) in enumerate((
            (rows_hbm, rows_ref), (w_hbm, w_ref), (gain_hbm, gain_ref), (bin_hbm, bin_ref),
            (cnt_hbm, cnt_ref), (own_hbm, own_ref), (loc_hbm, loc_ref), (logq_hbm, logq_ref),
            (q_hbm, q_ref), (lab_hbm, lab_ref),
        ))
    ]
    for fetch in fetches:
        fetch.start()

    me, t = lax.axis_index("dp"), lax.axis_index("table")
    y, c = lax.div(me, CORES), lax.rem(me, CORES)
    x, z = lax.div(t, n_z), lax.rem(t, n_z)
    sib = y * CORES + (1 - c)

    def at(y_pos, core):
        return lax.rem(y_pos + 2 * n_y, n_y) * CORES + core

    up, down = at(y + 1, c), at(y - 1, c)

    def turns(n):
        return [(i + 1) // 2 * (1 if i % 2 else -1) for i in range(n)]

    def dp_each(do):
        for off in turns(n_y):
            y_pos = lax.rem(y + (off + n_y), n_y) * CORES
            if off:
                do(y_pos + c)
            do(y_pos + (1 - c))

    def z_each(do):
        for off in turns(n_z)[1:]:
            do(lax.rem(z + (off + n_z), n_z))

    def x_each(do):
        for off in range(1, n_x):
            do(lax.rem(x + off, n_x))

    def tab_each(do):
        cols = [lax.rem(x + off, n_x) * n_z for off in range(n_x)]
        far = lax.rem(z + n_z // 2, n_z)
        for k, col in enumerate(cols):
            if k:
                do(col + z)
            do(col + far)

        def pair(m, _):
            ahead, behind = lax.rem(z + m, n_z), lax.rem(z + n_z - m, n_z)
            for col in cols:
                do(col + ahead)
                do(col + behind)
            return 0

        lax.fori_loop(1, n_z // 2, pair, 0)

    barrier = pltpu.get_barrier_semaphore()

    def greet(axis):
        return lambda peer: pl.semaphore_signal(
            barrier, inc=1, device_id={axis: peer}, device_id_type=MESH
        )

    dp_each(greet("dp"))
    tab_each(greet("table"))

    for fetch in fetches[:8]:
        fetch.wait()
    rows = rows_ref[...]
    blocks[me, :u_rows, :] = rows
    offs = split3(logq_ref[...] * (-1.0 / INV_TEMP))
    table = jnp.zeros((EXT, logq_ref.shape[1]), F32)
    for k, part in enumerate(offs):
        table = jnp.where(iota(table.shape, 0) == k, part, table)
    hits = (iota((logq_ref.shape[1], u_rows), 0) == bin_ref[...]).astype(F32).astype(BF16)
    ext = dot(table.astype(BF16), hits)
    line = iota(ext.shape, 0)
    dead = iota(ext.shape, 1) >= cnt_ref[...]
    ext = jnp.where(dead, jnp.where(line == 0, NEG, 0.0), ext)
    own, loc = own_ref[...], loc_ref[...]
    bits = n_tab.bit_length() - 1
    fields = (own >> bits, own & (n_tab - 1), loc >> 8, loc & 255)
    for k, part in enumerate(fields):
        ext = jnp.where(line == 3 + k, part.astype(F32), ext)
    blocks[me, u_rows:, :] = ext.astype(BF16)
    for fetch in fetches[8:]:
        fetch.wait()
    q_t[...] = q_ref[...].astype(F32).T.astype(BF16)
    z_t[...] = jnp.zeros_like(z_t)
    ring_in[1, 0, 1] = jnp.zeros((u_rows // 2, width), BF16)
    ring_in[0, 0, 0] = jnp.zeros((u_rows // 2, width), BF16)
    base_ref[...] = jnp.zeros_like(base_ref)

    before = (iota((u_rows, u_rows), 0) < iota((u_rows, u_rows), 1)).astype(F32).astype(BF16)
    own_dp = ext[3:4, :]
    is_dp = (iota((n_dp, u_rows), 0).astype(F32) == own_dp).astype(F32)
    rank = jnp.sum(is_dp * dot(is_dp.astype(BF16), before), axis=0, keepdims=True)
    pos = (own_dp * cap_dp + rank).astype(jnp.int32)
    place[...] = (iota((n_dp * cap_dp, u_rows), 0) == pos).astype(F32).astype(BF16)
    pl.semaphore_wait(barrier, n_dp + n_tab - 2)

    def ring_block(b, sub, d, way):
        return pltpu.make_async_remote_copy(
            src_ref=blocks.at[b, subs[sub]], dst_ref=blocks.at[b, subs[sub]],
            send_sem=ag_ring_send.at[way, d, sub], recv_sem=ag_ring_recv.at[b, sub],
            device_id={"dp": up if way else down}, device_id_type=MESH,
        )

    def to_sib(b):
        return pltpu.make_async_remote_copy(
            src_ref=blocks.at[b], dst_ref=blocks.at[b],
            send_sem=ag_sib_send.at[lax.div(b, CORES)], recv_sem=ag_sib_recv.at[lax.div(b, CORES)],
            device_id={"dp": sib}, device_id_type=MESH,
        )

    pick = (iota((EXT, q_rows), 0) < 3).astype(F32).astype(BF16)

    def score(b):
        rows = blocks[b, :u_rows, :]
        items = (gain_ref[...] * rows.astype(F32) + dot(rows, w_ref[...])).astype(BF16)
        raw = dot(items, q_t[...]) + dot(blocks[b, u_rows:, :], pick, 0, 0)
        high = jnp.max(raw, axis=0, keepdims=True)
        e = jnp.exp2((raw - high) * SCALE2)
        weights[b] = e
        top[b] = high
        total[b] = jnp.sum(e, axis=0, keepdims=True)

    def gather_step(d, _):
        near = (at(y + d, c), at(y - d, c))
        between = (d > 0) & (d < half)
        for sub in (0, 1):
            for way in (1, 0):
                b = near[way]

                @pl.when(between | ((d == half) & (sub == 1 - way)))
                def _():
                    ring_block(b, sub, 0, way).wait_recv()

                forward = d < half if sub == 1 - way else d < half - 1

                @pl.when(forward)
                def _():
                    ring_block(b, sub, d, way).start()

        to_sib(near[1]).start()

        @pl.when(between)
        def _():
            to_sib(near[0]).start()

        n = jnp.where((d == 0) | (d == half), 1, 2)

        def one(i, _):
            side, j = lax.div(i, n), lax.rem(i, n)
            b = at(y + (2 * j - 1) * d, jnp.where(side == 0, c, 1 - c))

            @pl.when(side == 1)
            def _():
                to_sib(b).wait_recv()

            score(b)
            return 0

        return lax.fori_loop(0, 2 * n, one, 0)

    lax.fori_loop(0, half + 1, gather_step, 0)

    high = jnp.max(top[...], axis=0)
    rel = jnp.exp2((top[...] - high[None]) * SCALE2)
    mass = jnp.sum(total[...] * rel, axis=0)
    top[...] = rel * (INV_TEMP / mass)[None]

    def sib_copy(slot):
        return pltpu.make_async_remote_copy(
            src_ref=sib_out.at[slot], dst_ref=sib_in.at[slot],
            send_sem=rs_sib_send.at[slot], recv_sem=rs_sib_recv.at[slot],
            device_id={"dp": sib}, device_id_type=MESH,
        )

    def ring_sum(way, k, sub):
        return pltpu.make_async_remote_copy(
            src_ref=ring_out.at[way, k, sub], dst_ref=ring_in.at[way, k, sub],
            send_sem=rs_ring_send.at[way, k, sub], recv_sem=rs_ring_recv.at[way, k, sub],
            device_id={"dp": up if way else down}, device_id_type=MESH,
        )

    def part_of(b):
        lab = jnp.where(b == me, lab_ref[...], -1)
        grad = weights[b] * top[b]
        grad = jnp.where(iota(grad.shape, 0) == lab, grad - INV_TEMP, grad).astype(BF16)
        z_t[...] += dot(blocks[b, :u_rows, :], grad, 0, 0)
        return dot(grad, q_ref[...])

    def event(e, core):
        d, j = half - lax.div(e + 1, 2), lax.rem(e + 1, 2)
        return at(y + (2 * j - 1) * d, core)

    def give_sib(e, _):
        sib_out[e] = part_of(event(e, 1 - c)).astype(BF16)
        sib_copy(e).start()
        return 0

    def take(e):
        part = part_of(event(e, c))
        sib_copy(e).wait_recv()
        return part + sib_in[e].astype(F32)

    DP, TAB, META, W, X, R, ROW, FULL = range(8)

    def send(kind, axis, peer, src, dst):
        pltpu.make_async_remote_copy(
            src_ref=src, dst_ref=dst, send_sem=all_send.at[kind], recv_sem=all_recv.at[kind],
            device_id={axis: peer}, device_id_type=MESH,
        ).start()

    def whole(kind, buf):
        part = buf.at[pl.ds(0, buf.shape[0] - 1)]
        return pltpu.make_async_remote_copy(
            src_ref=part, dst_ref=part, send_sem=all_send.at[kind], recv_sem=all_recv.at[kind],
            device_id={"dp": sib}, device_id_type=MESH,
        )

    me_f = me.astype(F32)
    per = 128 // cap_dp
    n_groups = n_dp // per
    tab_line = iota((n_tab, u_rows), 0).astype(F32)
    spot = iota((128, u_rows), 0).astype(F32)
    ext_line = iota((EXT, u_rows), 0)

    def arrivals(g, _):
        def one(i, carry):
            base, found = carry
            slot = blocks[g * per + i, u_rows:, :].astype(F32)
            here = (slot[3:4, :] == me_f).astype(F32)
            tab, row_hi, row_lo = slot[4:5, :], slot[5:6, :], slot[6:7, :]
            is_tab = jnp.where(tab_line == tab, here, 0.0)
            earlier = dot(is_tab.astype(BF16), before)
            order = jnp.sum(is_tab * (earlier + base), axis=0, keepdims=True)
            nth = jnp.sum(earlier, axis=0, keepdims=True) + (i * cap_dp).astype(F32)
            base = base + jnp.sum(is_tab, axis=1, keepdims=True)
            meta = jnp.zeros((EXT, u_rows), F32)
            for k, part in enumerate((here, tab, order, row_hi, row_lo)):
                meta = jnp.where(ext_line == k, part * here, meta)
            sel = jnp.where(spot == nth, here, 0.0)
            return base, found + dot(meta.astype(BF16), sel.astype(BF16), 1, 1)

        base, found = lax.fori_loop(0, per, one, (base_ref[...], jnp.zeros((EXT, 128), F32)))
        base_ref[...] = base
        mid_meta[:, pl.ds(pl.multiple_of(g * 128, 128), 128)] = found
        return 0

    def ring_step(k):
        for sub in (0, 1):
            for way in (1, 0):
                if k > 1 or sub == 1 - way:
                    ring_sum(way, k - 1, sub).wait_recv()
                so_far = acc[2 * k - 1 + way, halves[sub], :] + ring_in[way, k - 1, sub].astype(F32)
                ring_out[way, k, sub] = so_far.astype(BF16)
                ring_sum(way, k, sub).start()

    def keep(e, _):
        acc[e] = take(e)
        return 0

    give_sib(0, 0)
    far = take(0).astype(BF16)
    for way in (1, 0):
        ring_out[way, 0, 1 - way] = far[halves[1 - way].start : halves[1 - way].start + u_rows // 2]
        ring_sum(way, 0, 1 - way).start()
    lax.fori_loop(1, n_y, give_sib, 0)
    early = 1
    if half > 1:
        early = 3
        lax.fori_loop(1, early, keep, 0)
        ring_step(1)
    lax.fori_loop(early, n_y, keep, 0)

    z_hi = z_t[...].astype(BF16)
    z_low = (z_t[...] - z_hi.astype(F32)).astype(BF16)
    w_out[...] = (dot(z_hi, q_ref[...]) + dot(z_low, q_ref[...])).astype(BF16).reshape(w_out.shape)
    z_each(lambda p: send(W, "table", x * n_z + p, w_out.at[p], w_in.at[z]))
    w_in[z] = w_out[z]

    def sum_z():
        whole(W, w_in).wait_recv()
        x_in[x] = jnp.sum(w_in[...].astype(F32), axis=0)
        x_each(lambda p: send(X, "table", p * n_z + z, x_in.at[x], x_in.at[x]))

    def sum_x():
        whole(X, x_in).wait_recv()
        r_out[...] = jnp.sum(x_in[...], axis=0).reshape(r_out.shape)
        dp_each(lambda p: send(R, "dp", p, r_out.at[p], r_in.at[me]))
        r_in[me] = r_out[me]

    def some(first_group, last_group):
        lax.fori_loop(first_group, last_group, arrivals, 0)

    work = [
        lambda: (some(0, n_groups // 2), sum_z()),
        lambda: (some(n_groups // 2, n_groups), sum_x()),
    ]
    for k in range(2, half):
        ring_step(k)
        if work:
            work.pop(0)()
    for do in work:
        do()

    for sub in (0, 1):
        for way in (1, 0):
            if sub == 1 - way or half > 1:
                ring_sum(way, half - 1, sub).wait_recv()
    for sub in (0, 1):
        arrived = ring_in[0, half - 1, sub].astype(F32) + ring_in[1, half - 1, sub].astype(F32)
        acc[n_y - 1, halves[sub], :] += arrived
    ig = acc[n_y - 1]
    row_grad = (gain_ref[...] * ig + dot(ig.astype(BF16), w_ref[...], 1, 1)).astype(BF16)
    first[...] = dot(place[...], row_grad).astype(BF16).reshape(first.shape)
    dp_each(lambda p: send(DP, "dp", p, first.at[p], mid.at[me]))
    mid[me] = first[me]

    n_mid = n_dp * cap_dp
    meta = mid_meta[...]
    valid, tab, order, row_hi, row_lo = (meta[k : k + 1, :] for k in range(5))
    tab = jnp.where(valid > 0.5, tab, -1.0)
    is_tab = iota((n_tab, n_mid), 0).astype(F32) == tab
    is_order = (iota((128, n_mid), 0).astype(F32) == order).astype(F32).astype(BF16)

    def spread(value):
        return dot(jnp.where(is_tab, value, 0.0).astype(BF16), is_order, 1, 1)

    code = 256.0 * spread(row_hi) + spread(row_lo) + spread(valid) - 1.0
    meta_out[...] = code.reshape(meta_out.shape)
    tab_each(lambda p: send(META, "table", p, meta_out.at[p], meta_in.at[t]))
    meta_in[t] = meta_out[t]

    whole(R, r_in).wait_recv()
    row_in[me] = jnp.sum(r_in[...], axis=0) * (1.0 / queries_all)
    dp_each(lambda p: send(ROW, "dp", p, row_in.at[me], row_in.at[me]))

    pos2 = (tab * cap_t + order).astype(jnp.int32)
    place2 = (iota((n_tab * cap_t, n_mid), 0) == pos2).astype(F32).astype(BF16)

    whole(DP, mid).wait_recv()
    out = dot(place2, mid[...].reshape(n_mid, width)).reshape(n_tab, cap_t, width)
    second[:, :cap_t, :] = out[:, :, :128].astype(BF16)
    second[:, cap_t:, :] = out[:, :, 128:].astype(BF16)
    tab_each(lambda p: send(TAB, "table", p, second.at[p], got.at[t]))
    got[t] = second[t]

    whole(ROW, row_in).wait_recv()
    full[z] = row_in[...]
    z_each(lambda p: send(FULL, "table", x * n_z + p, full.at[z], full.at[z]))

    z_all = z_t[...].T
    z_hi = z_all.astype(BF16)
    z_low = (z_all - z_hi.astype(F32)).astype(BF16)
    gq_ref[...] = (gain_ref[...] * z_all + dot(z_hi, w_ref[...]) + dot(z_low, w_ref[...])).astype(BF16)
    gq_copy = pltpu.make_async_copy(gq_ref, gq_hbm, out_sem.at[0])
    gq_copy.start()

    whole(META, meta_in).wait_recv()
    code = meta_in[...].reshape(n_tab, 128).astype(jnp.int32) + 1
    n_got = n_tab * cap_t
    cols = iota((1, n_got), 1)
    is_src = (iota((n_tab, n_got), 0) == lax.div(iota((n_tab, n_got), 1), cap_t)).astype(F32).astype(BF16)

    def along(value):
        return dot(value.astype(F32).astype(BF16), is_src, 0, 0)

    wide = 256.0 * along(code >> 8) + along(code & 255) - 1.0
    mine = iota((128, n_got), 0) == lax.rem(cols, cap_t)
    code_ref[...] = jnp.sum(jnp.where(mine, wide, 0.0), axis=0, keepdims=True).astype(jnp.int32)
    code_copy = pltpu.make_async_copy(code_ref, code_hbm, out_sem.at[1])
    code_copy.start()

    for d in range(half):
        for way in (0, 1):
            for sub in (0, 1):
                if sub == 1 - way or d < half - 1:
                    ring_block(me, sub, d, way).wait_send()
                if sub == 1 - way or d > 0:
                    ring_sum(way, d, sub).wait_send()
    for k in range(n_y):
        to_sib(k * CORES).wait_send()
        sib_copy(k).wait_send()
    for kind, buf in ((W, w_in), (X, x_in), (R, r_in), (ROW, row_in), (META, meta_in), (DP, mid)):
        whole(kind, buf).wait_send()

    whole(FULL, full).wait_recv()
    gw = full[...].reshape(width, width)
    gw_ref[...] = gw
    gw_copy = pltpu.make_async_copy(gw_ref, gw_hbm, out_sem.at[2])
    gw_copy.start()
    diag = iota((width, width), 0) == iota((width, width), 1)
    gg_ref[...] = jnp.sum(jnp.where(diag, gw, 0.0), axis=0, keepdims=True)
    gg_copy = pltpu.make_async_copy(gg_ref, gg_hbm, out_sem.at[3])
    gg_copy.start()

    whole(TAB, got).wait_recv()
    arrived = got[...].astype(F32)
    got_ref[:, :128] = arrived[:, :cap_t, :].reshape(n_got, 128).astype(BF16)
    got_ref[:, 128:] = arrived[:, cap_t:, :].reshape(n_got, 128).astype(BF16)
    got_copy = pltpu.make_async_copy(got_ref, got_hbm, out_sem.at[4])
    got_copy.start()
    whole(TAB, got).wait_send()
    whole(FULL, full).wait_send()
    for copy in (gq_copy, code_copy, gw_copy, gg_copy, got_copy):
        copy.wait()


def step(n_dp, n_x, n_z, queries, item_rows, item_bin, counts, labels, owner, local_row, logq, w, gain):
    q_rows, width = queries.shape
    u_rows = item_rows.shape[0]
    n_tab = n_x * n_z
    n_y = n_dp // CORES
    half = n_y // 2
    cap_dp = max(2, 2 * u_rows // n_dp)
    cap_t = max(2, (n_dp * cap_dp + n_tab - 1) // n_tab)
    z_rows = width // n_z
    r_rows = z_rows // n_dp
    args = (
        queries, item_rows, item_bin[None], counts[None], labels[None], owner[None], local_row[None],
        logq[None], w, gain[None],
    )
    outs = (
        jax.ShapeDtypeStruct((q_rows, width), BF16),
        jax.ShapeDtypeStruct((n_tab * cap_t, width), BF16),
        jax.ShapeDtypeStruct((1, n_tab * cap_t), jnp.int32),
        jax.ShapeDtypeStruct((width, width), F32),
        jax.ShapeDtypeStruct((1, width), F32),
    )
    vmem = pltpu.VMEM
    sem = pltpu.SemaphoreType.DMA
    return pl.pallas_call(
        functools.partial(step_kernel, n_dp, n_x, n_z, cap_dp, cap_t),
        out_shape=outs,
        in_specs=[pl.BlockSpec(memory_space=pl.ANY)] * len(args),
        out_specs=(pl.BlockSpec(memory_space=pl.ANY),) * len(outs),
        scratch_shapes=[vmem(a.shape, a.dtype) for a in args + outs]
        + [
            vmem((n_dp, u_rows + EXT, width), BF16),
            vmem((n_dp, u_rows, q_rows), F32),
            vmem((width, q_rows), BF16),
            vmem((width, q_rows), F32),
            vmem((n_dp, 1, q_rows), F32),
            vmem((n_dp, 1, q_rows), F32),
            vmem((n_y, u_rows, width), F32),
            vmem((n_y, u_rows, width), BF16),
            vmem((n_y, u_rows, width), BF16),
            vmem((2, half, 2, u_rows // 2, width), BF16),
            vmem((2, half, 2, u_rows // 2, width), BF16),
            vmem((EXT, n_dp * cap_dp), F32),
            vmem((n_tab, 1), F32),
            vmem((n_dp * cap_dp, u_rows), BF16),
            vmem((n_dp, cap_dp, width), BF16),
            vmem((n_dp, cap_dp, width), BF16),
            vmem((n_tab, 2 * cap_t, 128), BF16),
            vmem((n_tab, 2 * cap_t, 128), BF16),
            vmem((n_tab, 1, 128), F32),
            vmem((n_tab, 1, 128), F32),
            vmem((n_z, z_rows, width), BF16),
            vmem((n_z, z_rows, width), BF16),
            vmem((n_x, z_rows, width), F32),
            vmem((n_dp, r_rows, width), F32),
            vmem((n_dp, r_rows, width), F32),
            vmem((n_dp, r_rows, width), F32),
            vmem((n_z, n_dp, r_rows, width), F32),
            sem((len(args),)), sem((len(outs),)),
            sem((2, half, 2)), sem((n_dp, 2)), sem((n_y,)), sem((n_y,)),
            sem((n_y,)), sem((n_y,)), sem((2, half, 2)), sem((2, half, 2)),
            sem((8,)), sem((8,)),
        ],
        compiler_params=pltpu.CompilerParams(
            collective_id=0, has_side_effects=True, vmem_limit_bytes=60 << 20
        ),
        name="group_step",
    )(*args)


def place_kernel(got_ref, code_ref, gq_in, gw_in, gg_in, out_ref, gq_ref, gw_ref, gg_ref):
    tile = out_ref.shape[0]
    line = iota((tile, code_ref.shape[1]), 0) + pl.program_id(0) * tile
    hits = (line == code_ref[...]).astype(F32).astype(BF16)
    out_ref[...] = dot(hits, got_ref[...])

    @pl.when(pl.program_id(0) == 0)
    def _():
        gq_ref[...] = gq_in[...]
        gw_ref[...] = gw_in[...]
        gg_ref[...] = gg_in[...]


def place_rows(got, code, *others):
    tile = 512
    n_got, width = got.shape
    whole = lambda a: pl.BlockSpec(a.shape, lambda i: (0, 0))
    return pl.pallas_call(
        place_kernel,
        grid=(ROWS_DEV // tile,),
        out_shape=(jax.ShapeDtypeStruct((ROWS_DEV, width), F32),)
        + tuple(jax.ShapeDtypeStruct(a.shape, a.dtype) for a in others),
        in_specs=[whole(a) for a in (got, code, *others)],
        out_specs=(pl.BlockSpec((tile, width), lambda i: (i, 0)),) + tuple(whole(a) for a in others),
        compiler_params=pltpu.CompilerParams(vmem_limit_bytes=32 << 20),
        name="place_rows",
    )(got, code, *others)


def body(n_dp, n_x, n_z, *args):
    grad_query, got, code, gw, gg = step(n_dp, n_x, n_z, *args)
    grad_table, grad_query, gw, gg = place_rows(got, code, grad_query, gw, gg)
    return grad_query, grad_table, gw, gg.reshape(-1)


def solution(mesh):
    n_x = X_CHIPS
    split = P(("dp", "table"))
    split2 = P(("dp", "table"), None)
    return jax.shard_map(
        functools.partial(body, mesh.shape["dp"], n_x, mesh.shape["table"] // n_x),
        mesh=mesh,
        in_specs=(split2, split2, split, split, split, split, split, P(), P(), P()),
        out_specs=(split2, split2, P(), P()),
        check_vma=False,
    )
```

time: 832 us -> 117 us (0.14)
  waiting for transfers between devices: 367 us -> 0 us
  local copies, waits for them, and re-layouts: 190 us -> 4.15 us
  blocking collectives: 164 us -> 0 us
  Pallas kernels: 0 us -> 111 us
  starting transfers between devices: 47.3 us -> 0 us
  other arithmetic: 27.9 us -> 0 us
  matrix products: 15.3 us -> 0 us
  between operations: 14.6 us -> 1.3 us
    psum x1 -> x0, waiting for transfers between devices: 352 us -> none  [body(): weight_sum, gain_sum = lax.psum((weight_part, gain_part), ('dp', 'table'))]
    scatter x5 -> x0, local copies, waits for them, and re-layouts: 179 us -> none  [the longest x1 56.2 us: body(): second_grad = jnp.zeros((n_tab, cap_tab, width), jnp.bfloat16).at[mid_tab...]
    psum x1 -> x0, blocking collectives: 122 us -> none  [body(): weight_sum, gain_sum = lax.psum((weight_part, gain_part), ('dp', 'table'))]
    pallas_call x0 -> x2, Pallas kernels: none -> 111 us  [the longest x1 108 us: step(): pl.pallas_call(functools.partial(step_kernel, n_dp, n_x, n_z, cap_dp, cap...]
    all_to_all x5 -> x0, starting transfers between devices: 47.2 us -> none  [the longest x1 16.3 us: body(): lax.all_to_all(second_rows, 'table', split_axis=0, concat_axis=0, tiled=T...]
    all_gather x1 -> x0, blocking collectives: 25.6 us -> none  [body(): lax.all_gather(item_bin, 'dp', axis=0, tiled=True)]
    unnamed x1 -> x0, blocking collectives: 16.3 us -> none
    dot_general x6 -> x0, matrix products: 15.3 us -> none  [the longest x1 4.24 us: body(): jnp.dot(logit_grad, group_v, preferred_element_type=jnp.float32)]
  transfers between devices with their start and end apart: 8 -> 0, of which waited for: 3 -> 0; matrix products, arithmetic and copies ran while one was open for 19% -> 0% of each run, Pallas kernels for 0% -> 0%
where the time goes in v1:
time: 117 us; the launch traced here: 116 us
  Pallas kernels  111 us (95%)
  local copies, waits for them, and re-layouts  4.15 us (4%)
  between operations  1.3 us (1%)
    pallas_call x1, Pallas kernels, step(): pl.pallas_call(functools.partial(step_kernel, n_dp, n_x, n_z, cap_dp, cap...  108 us
    unnamed x10, local copies, waits for them, and re-layouts  4.15 us
    pallas_call x1, Pallas kernels, place_rows(): pl.pallas_call(place_kernel, grid=(ROWS_DEV // tile,), out_shape=(jax.Sha...  2.7 us

profile of v1, /device:TPU:1, one launch (start us, length us, event | category | flops | bytes accessed | tf_op | source)
XLA Modules:
  0.0 116.5 jit_solution(14704377784295735554)
XLA Ops:
  1.3 108.3 %group_step.1 = (bf16[512,256]{1,0:T(8,128)(2,1)}, bf16[512,256]{1,0:T(8,128)(2,1)}, s32[1,512]{1,0:T(1,128)}, f32[256,256]{1,0:T(8,128)}, f32[1,256]{1,0:T(1,128)}) custom-call(bf16[512,256]{1,0:T(8,128)(2,1)} %q_hbm.1, bf16[256,256]{1,0:T(8,128)(2,1)} %rows_hbm.1, s32[1,256]{1,0:T(1,128)} %bitcast.10, s32[1,1]{1,0:T(1,128)} %bitcast.8.cnt_hbm, ...), custom_call_target="tpu_custom_call" | custom-call | tf_op jit(solution)/shard_map/group_step/pallas_call | solution.py:495
  109.6 0.0 copy-start
  109.6 0.9 copy-done
  110.6 0.0 copy-start.1
  110.6 0.9 copy-done.1
  111.5 0.0 copy-start.2
  111.5 0.9 copy-done.2
  112.5 0.0 copy-start.3
  112.5 0.7 copy-done.3
  113.2 0.0 copy-start.4
  113.2 0.6 copy-done.4
  113.8 2.7 %place_rows.1 = (f32[2048,256]{1,0:T(8,128)}, bf16[512,256]{1,0:T(8,128)(2,1)}, f32[256,256]{1,0:T(8,128)}, f32[1,256]{1,0:T(1,128)}) custom-call(bf16[512,256]{1,0:T(8,128)(2,1)S(1)} %copy-done.1, s32[1,512]{1,0:T(1,128)S(1)} %copy-done.3, bf16[512,256]{1,0:T(8,128)(2,1)S(1)} %copy-done, f32[256,256]{1,0:T(8,128)S(1)} %copy-done.2, f32[1,256]{1,0:T(1,128)S(1)} %copy-done.4), custom_call_target="tpu_custom_call" | custom-call | tf_op jit(solution)/shard_map/place_rows/pallas_call | solution.py:558
Async XLA Ops:
  109.6 1.0 copy-start
  110.6 0.9 copy-start.1
  111.5 0.9 copy-start.2
  112.5 0.7 copy-start.3
  113.2 0.6 copy-start.4

commit v2 on v1

--- a/solution.py
+++ b/solution.py
@@ -208,22 +208,32 @@
         def _():
             to_sib(near[0]).start()
 
-        n = jnp.where((d == 0) | (d == half), 1, 2)
-
-        def one(i, _):
-            side, j = lax.div(i, n), lax.rem(i, n)
-            b = at(y + (2 * j - 1) * d, jnp.where(side == 0, c, 1 - c))
-
-            @pl.when(side == 1)
-            def _():
-                to_sib(b).wait_recv()
-
+        def one(j, _):
+            score(at(y + (2 * j - 1) * d, c))
+            return 0
+
+        lax.fori_loop(0, ways(d), one, 0)
+
+        @pl.when(d > 0)
+        def _():
+            from_sib(d - 1)
+
+        return 0
+
+    def ways(d):
+        return jnp.where((d == 0) | (d == half), 1, 2)
+
+    def from_sib(d):
+        def one(j, _):
+            b = at(y + (2 * j - 1) * d, 1 - c)
+            to_sib(b).wait_recv()
             score(b)
             return 0
 
-        return lax.fori_loop(0, 2 * n, one, 0)
+        lax.fori_loop(0, ways(d), one, 0)
 
     lax.fori_loop(0, half + 1, gather_step, 0)
+    from_sib(half)
 
     high = jnp.max(top[...], axis=0)
     rel = jnp.exp2((top[...] - high[None]) * SCALE2)
@@ -338,26 +348,26 @@
     z_hi = z_t[...].astype(BF16)
     z_low = (z_t[...] - z_hi.astype(F32)).astype(BF16)
     w_out[...] = (dot(z_hi, q_ref[...]) + dot(z_low, q_ref[...])).astype(BF16).reshape(w_out.shape)
-    z_each(lambda p: send(W, "table", x * n_z + p, w_out.at[p], w_in.at[z]))
-    w_in[z] = w_out[z]
+    dp_each(lambda p: send(W, "dp", p, w_out.at[p], w_in.at[me]))
+    w_in[me] = w_out[me]
+
+    def sum_dp():
+        whole(W, w_in).wait_recv()
+        r_out[...] = jnp.sum(w_in[...].astype(F32), axis=0).reshape(r_out.shape)
+        z_each(lambda p: send(R, "table", x * n_z + p, r_out.at[p], r_in.at[z]))
+        r_in[z] = r_out[z]
 
     def sum_z():
-        whole(W, w_in).wait_recv()
-        x_in[x] = jnp.sum(w_in[...].astype(F32), axis=0)
+        whole(R, r_in).wait_recv()
+        x_in[x] = jnp.sum(r_in[...], axis=0)
         x_each(lambda p: send(X, "table", p * n_z + z, x_in.at[x], x_in.at[x]))
-
-    def sum_x():
-        whole(X, x_in).wait_recv()
-        r_out[...] = jnp.sum(x_in[...], axis=0).reshape(r_out.shape)
-        dp_each(lambda p: send(R, "dp", p, r_out.at[p], r_in.at[me]))
-        r_in[me] = r_out[me]
 
     def some(first_group, last_group):
         lax.fori_loop(first_group, last_group, arrivals, 0)
 
     work = [
-        lambda: (some(0, n_groups // 2), sum_z()),
-        lambda: (some(n_groups // 2, n_groups), sum_x()),
+        lambda: (some(0, n_groups // 2), sum_dp()),
+        lambda: (some(n_groups // 2, n_groups), sum_z()),
     ]
     for k in range(2, half):
         ring_step(k)
@@ -379,6 +389,10 @@
     dp_each(lambda p: send(DP, "dp", p, first.at[p], mid.at[me]))
     mid[me] = first[me]
 
+    whole(X, x_in).wait_recv()
+    row_in[z] = jnp.sum(x_in[...], axis=0) * (1.0 / queries_all)
+    z_each(lambda p: send(ROW, "table", x * n_z + p, row_in.at[z], row_in.at[z]))
+
     n_mid = n_dp * cap_dp
     meta = mid_meta[...]
     valid, tab, order, row_hi, row_lo = (meta[k : k + 1, :] for k in range(5))
@@ -394,10 +408,6 @@
     tab_each(lambda p: send(META, "table", p, meta_out.at[p], meta_in.at[t]))
     meta_in[t] = meta_out[t]
 
-    whole(R, r_in).wait_recv()
-    row_in[me] = jnp.sum(r_in[...], axis=0) * (1.0 / queries_all)
-    dp_each(lambda p: send(ROW, "dp", p, row_in.at[me], row_in.at[me]))
-
     pos2 = (tab * cap_t + order).astype(jnp.int32)
     place2 = (iota((n_tab * cap_t, n_mid), 0) == pos2).astype(F32).astype(BF16)
 
@@ -409,8 +419,8 @@
     got[t] = second[t]
 
     whole(ROW, row_in).wait_recv()
-    full[z] = row_in[...]
-    z_each(lambda p: send(FULL, "table", x * n_z + p, full.at[z], full.at[z]))
+    full[me] = row_in[...]
+    dp_each(lambda p: send(FULL, "dp", p, full.at[me], full.at[me]))
 
     z_all = z_t[...].T
     z_hi = z_all.astype(BF16)
@@ -477,8 +487,8 @@
     half = n_y // 2
     cap_dp = max(2, 2 * u_rows // n_dp)
     cap_t = max(2, (n_dp * cap_dp + n_tab - 1) // n_tab)
-    z_rows = width // n_z
-    r_rows = z_rows // n_dp
+    w_rows = width // n_dp
+    r_rows = w_rows // n_z
     args = (
         queries, item_rows, item_bin[None], counts[None], labels[None], owner[None], local_row[None],
         logq[None], w, gain[None],
@@ -519,13 +529,13 @@
             vmem((n_tab, 2 * cap_t, 128), BF16),
             vmem((n_tab, 1, 128), F32),
             vmem((n_tab, 1, 128), F32),
-            vmem((n_z, z_rows, width), BF16),
-            vmem((n_z, z_rows, width), BF16),
-            vmem((n_x, z_rows, width), F32),
-            vmem((n_dp, r_rows, width), F32),
-            vmem((n_dp, r_rows, width), F32),
-            vmem((n_dp, r_rows, width), F32),
-            vmem((n_z, n_dp, r_rows, width), F32),
+            vmem((n_dp, w_rows, width), BF16),
+            vmem((n_dp, w_rows, width), BF16),
+            vmem((n_x, r_rows, width), F32),
+            vmem((n_z, r_rows, width), F32),
+            vmem((n_z, r_rows, width), F32),
+            vmem((n_z, r_rows, width), F32),
+            vmem((n_dp, n_z, r_rows, width), F32),
             sem((len(args),)), sem((len(outs),)),
             sem((2, half, 2)), sem((n_dp, 2)), sem((n_y,)), sem((n_y,)),
             sem((n_y,)), sem((n_y,)), sem((2, half, 2)), sem((2, half, 2)),
@@ -562,7 +572,7 @@
         + tuple(jax.ShapeDtypeStruct(a.shape, a.dtype) for a in others),
         in_specs=[whole(a) for a in (got, code, *others)],
         out_specs=(pl.BlockSpec((tile, width), lambda i: (i, 0)),) + tuple(whole(a) for a in others),
-        compiler_params=pltpu.CompilerParams(vmem_limit_bytes=32 << 20),
+        compiler_params=pltpu.CompilerParams(vmem_limit_bytes=60 << 20),
         name="place_rows",
     )(got, code, *others)
 

time: 117 us -> 100 us (0.85)
  Pallas kernels: 111 us -> 98.7 us
  local copies, waits for them, and re-layouts: 4.15 us -> 0 us
    pallas_call x1, Pallas kernels: 108 us -> 94.8 us  [step(): pl.pallas_call(functools.partial(step_kernel, n_dp, n_x, n_z, cap_dp, cap...]
    unnamed x10 -> x0, local copies, waits for them, and re-layouts: 4.15 us -> none
where the time goes in v2:
time: 100 us
  Pallas kernels  98.7 us (99%)
  between operations  1.29 us (1%)
    pallas_call x1, Pallas kernels, step(): pl.pallas_call(functools.partial(step_kernel, n_dp, n_x, n_z, cap_dp, cap...  94.8 us
    pallas_call x1, Pallas kernels, place_rows(): pl.pallas_call(place_kernel, grid=(ROWS_DEV // tile,), out_shape=(jax.Sha...  3.86 us

profile of v2, /device:TPU:1, one launch (start us, length us, event | category | flops | bytes accessed | tf_op | source)
XLA Modules:
  0.0 100.0 jit_solution(4628659401245922567)
XLA Ops:
  1.3 94.8 %group_step.1 = (bf16[512,256]{1,0:T(8,128)(2,1)}, bf16[512,256]{1,0:T(8,128)(2,1)}, s32[1,512]{1,0:T(1,128)}, f32[256,256]{1,0:T(8,128)}, f32[1,256]{1,0:T(1,128)}) custom-call(bf16[512,256]{1,0:T(8,128)(2,1)} %q_hbm.1, bf16[256,256]{1,0:T(8,128)(2,1)} %rows_hbm.1, s32[1,256]{1,0:T(1,128)} %bitcast.10, s32[1,1]{1,0:T(1,128)} %bitcast.8.cnt_hbm, ...), custom_call_target="tpu_custom_call" | custom-call | tf_op jit(solution)/shard_map/group_step/pallas_call | solution.py:505
  96.1 3.9 %place_rows.1 = (f32[2048,256]{1,0:T(8,128)}, bf16[512,256]{1,0:T(8,128)(2,1)}, f32[256,256]{1,0:T(8,128)}, f32[1,256]{1,0:T(1,128)}) custom-call(bf16[512,256]{1,0:T(8,128)(2,1)} %get-tuple-element.13.got_ref, s32[1,512]{1,0:T(1,128)} %get-tuple-element.14.code_ref, bf16[512,256]{1,0:T(8,128)(2,1)} %get-tuple-element.15.gq_in, ...), custom_call_target="tpu_custom_call" | custom-call | tf_op jit(solution)/shard_map/place_rows/pallas_call | solution.py:568

commit v3 on v2

--- a/solution.py
+++ b/solution.py
@@ -306,7 +306,7 @@
             is_tab = jnp.where(tab_line == tab, here, 0.0)
             earlier = dot(is_tab.astype(BF16), before)
             order = jnp.sum(is_tab * (earlier + base), axis=0, keepdims=True)
-            nth = jnp.sum(earlier, axis=0, keepdims=True) + (i * cap_dp).astype(F32)
+            nth = jnp.sum(earlier, axis=0, keepdims=True) + float(i * cap_dp)
             base = base + jnp.sum(is_tab, axis=1, keepdims=True)
             meta = jnp.zeros((EXT, u_rows), F32)
             for k, part in enumerate((here, tab, order, row_hi, row_lo)):
@@ -314,7 +314,10 @@
             sel = jnp.where(spot == nth, here, 0.0)
             return base, found + dot(meta.astype(BF16), sel.astype(BF16), 1, 1)
 
-        base, found = lax.fori_loop(0, per, one, (base_ref[...], jnp.zeros((EXT, 128), F32)))
+        found = (base_ref[...], jnp.zeros((EXT, 128), F32))
+        for i in range(per):
+            found = one(i, found)
+        base, found = found
         base_ref[...] = base
         mid_meta[:, pl.ds(pl.multiple_of(g * 128, 128), 128)] = found
         return 0

time: 100 us -> 100 us (level)
  no operation moved by 1% of the time
where the time goes in v3:
time: 100 us
  Pallas kernels  98.7 us (99%)
  between operations  1.29 us (1%)
    pallas_call x1, Pallas kernels, step(): pl.pallas_call(functools.partial(step_kernel, n_dp, n_x, n_z, cap_dp, cap...  94.8 us
    pallas_call x1, Pallas kernels, place_rows(): pl.pallas_call(place_kernel, grid=(ROWS_DEV // tile,), out_shape=(jax.Sha...  3.86 us

profile of v3, /device:TPU:1, one launch (start us, length us, event | category | flops | bytes accessed | tf_op | source)
XLA Modules:
  0.0 100.0 jit_solution(13139633002326704749)
XLA Ops:
  1.3 94.8 %group_step.1 = (bf16[512,256]{1,0:T(8,128)(2,1)}, bf16[512,256]{1,0:T(8,128)(2,1)}, s32[1,512]{1,0:T(1,128)}, f32[256,256]{1,0:T(8,128)}, f32[1,256]{1,0:T(1,128)}) custom-call(bf16[512,256]{1,0:T(8,128)(2,1)} %q_hbm.1, bf16[256,256]{1,0:T(8,128)(2,1)} %rows_hbm.1, s32[1,256]{1,0:T(1,128)} %bitcast.10, s32[1,1]{1,0:T(1,128)} %bitcast.8.cnt_hbm, ...), custom_call_target="tpu_custom_call" | custom-call | tf_op jit(solution)/shard_map/group_step/pallas_call | solution.py:508
  96.1 3.9 %place_rows.1 = (f32[2048,256]{1,0:T(8,128)}, bf16[512,256]{1,0:T(8,128)(2,1)}, f32[256,256]{1,0:T(8,128)}, f32[1,256]{1,0:T(1,128)}) custom-call(bf16[512,256]{1,0:T(8,128)(2,1)} %get-tuple-element.13.got_ref, s32[1,512]{1,0:T(1,128)} %get-tuple-element.14.code_ref, bf16[512,256]{1,0:T(8,128)(2,1)} %get-tuple-element.15.gq_in, ...), custom_call_target="tpu_custom_call" | custom-call | tf_op jit(solution)/shard_map/place_rows/pallas_call | solution.py:571
